TPU v7x, 32 devices: a whole 2x2x4 slice. The times are simulated.
32 devices in a mesh: elem: 32 (over z, y, x, core).
Axes of the slice: x: 2, y: 2, z: 4, core: 2. Of those that a mesh axis runs over, the one named last changes fastest.
Arguments:
- tracer: float32 [256, 8, 640], P('elem'), may hold values from 0 to 1
- old_mass: float32 [256, 128], P('elem'), may hold values from 0.3 to 3
- new_mass: float32 [256, 128], P('elem'), may hold values from 0.3 to 3
- dep_owner: int32 [256, 128, 1], P('elem'), may hold values from 0 to 31, as said below
- dep_local: int32 [256, 128], P('elem'), may hold values from 0 to 7
- dep_coord: float32 [2, 256, 128], P(None, 'elem'), may hold values from -1 to 1
Outputs:
- new_tracer: float32 [256, 8, 640], P('elem')
Inputs may be any that keep to these rules, and one draw needn't show every extreme that they name: `dep_owner`: the rows of one device name their own device or one of at most five other devices; no other device is named more than 32 times among them, and one other device is named exactly 32 times.
All inputs are finite; a program needn't handle non-finite values.
Results may differ from a plain program's by a relative error of at most 0.0003.
Values sent between devices are 32-bit elements; how exact they have to be, the bound alone decides.
A program may use at most 64 MiB of HBM per device.

v0:
```python
import math

import jax
import jax.numpy as jnp
from jax import lax
from jax.sharding import PartitionSpec as P

GLL_NODES = (-1.0, -0.4472135954999579, 0.4472135954999579, 1.0)


def one_axis(coord):
    columns = []
    for node_own in range(4):
        factor = jnp.ones_like(coord)
        for node_other in range(4):
            if node_other != node_own:
                factor = (
                    factor
                    * (coord - GLL_NODES[node_other])
                    / (GLL_NODES[node_own] - GLL_NODES[node_other])
                )
        columns.append(factor)
    return jnp.stack(columns, axis=-1)


def lagrange_weights(coord_a, coord_b):
    weights_a = one_axis(coord_a)
    weights_b = one_axis(coord_b)
    return (weights_a[..., :, None] * weights_b[..., None, :]).reshape(coord_a.shape + (16,))


def bound_terms(interp, lowest, highest):
    clipped = jnp.clip(interp, lowest, highest)
    margin = 0.01 + 0.05 * (highest - lowest)
    upper = highest + margin - clipped
    lower = clipped - lowest + margin
    return (clipped, upper, lower)


def fixer_terms(interp, lowest, highest, mass_new):
    clipped, upper, lower = bound_terms(interp, lowest, highest)
    sums = (
        jnp.sum(mass_new * clipped, axis=(0, 2)),
        jnp.sum(mass_new * upper, axis=(0, 2)),
        jnp.sum(mass_new * lower, axis=(0, 2)),
    )
    return (clipped, upper, lower, sums)


def apply_fix(clipped, upper, lower, source_total, clip_total, up_total, down_total):
    deficit = (source_total - clip_total)[:, None, :]
    return (
        clipped
        + jnp.maximum(deficit, 0.0) / up_total[:, None, :] * upper
        + jnp.minimum(deficit, 0.0) / down_total[:, None, :] * lower
    )


def body(tracer, old_mass, new_mass, dep_owner, dep_local, dep_coord):
    devices_count = lax.axis_size("elem")
    myself = lax.axis_index("elem")
    elems, levels, width = tracer.shape
    nodes = 16
    tracers = width // nodes
    total_rows = elems * levels * nodes
    capacity = total_rows // 32
    owner_flat = dep_owner.reshape(total_rows)
    is_home = owner_flat == myself
    level_index = jnp.broadcast_to(
        (jnp.arange(levels * nodes, dtype=jnp.int32) // nodes)[None, :], (elems, levels * nodes)
    ).reshape(total_rows)
    row_index = dep_local.reshape(total_rows) * levels + level_index
    peer_ids = jnp.arange(devices_count, dtype=jnp.int32)
    one_hot = (
        (owner_flat[:, None] == peer_ids[None, :]) & jnp.logical_not(is_home)[:, None]
    ).astype(jnp.int32)
    slot_index = jnp.sum(one_hot * (jnp.cumsum(one_hot, axis=0) - 1), axis=1)
    send_owner = jnp.where(is_home, devices_count, owner_flat)
    coord_a = dep_coord[0].reshape(total_rows)
    coord_b = dep_coord[1].reshape(total_rows)
    payload = jnp.stack([coord_a, coord_b], axis=-1)
    send_rows = (
        jnp.zeros((devices_count, capacity), jnp.int32)
        .at[send_owner, slot_index]
        .set(row_index, mode="drop")
    )
    send_load = (
        jnp.zeros((devices_count, capacity, payload.shape[-1]), jnp.float32)
        .at[send_owner, slot_index]
        .set(payload, mode="drop")
    )
    table_rows = elems * levels
    node_table = tracer.reshape(table_rows * nodes, tracers)
    per_node = tracer.reshape(table_rows, nodes, tracers)
    bounds_table = jnp.concatenate([jnp.min(per_node, axis=1), jnp.max(per_node, axis=1)], axis=-1)
    cell_ids = jnp.arange(table_rows, dtype=jnp.int32)
    shape4 = (elems, levels, nodes, tracers)
    mass_old = old_mass.reshape(elems, levels, nodes, 1)
    mass_new = new_mass.reshape(elems, levels, nodes, 1)
    local_source = jnp.sum(mass_old * tracer.reshape(shape4), axis=(0, 2))

    def evaluate_rows(rows, load):
        leading = rows.shape
        flat_rows = rows.reshape(-1)
        flat_load = load.reshape(-1, load.shape[-1])
        count = flat_rows.shape[0]
        weights = lagrange_weights(flat_load[:, 0], flat_load[:, 1])
        step_rows = math.gcd(count, 512)

        def one_block(inputs):
            block_rows, block_weights = inputs
            selector = (block_rows[:, None] == cell_ids[None, :]).astype(jnp.float32)
            spread = (selector[:, :, None] * block_weights[:, None, :]).reshape(
                step_rows, table_rows * nodes
            )
            values = jnp.dot(spread, node_table, precision=lax.Precision.HIGHEST)
            bounds = jnp.dot(selector, bounds_table, precision=lax.Precision.HIGHEST)
            return jnp.concatenate([values, bounds], axis=-1)

        blocks = lax.map(
            one_block,
            (
                flat_rows.reshape(count // step_rows, step_rows),
                weights.reshape(count // step_rows, step_rows, nodes),
            ),
        )
        return blocks.reshape(leading + (3 * tracers,))

    home_combined = evaluate_rows(row_index, payload)
    recv_rows = lax.all_to_all(send_rows, "elem", split_axis=0, concat_axis=0, tiled=True)
    recv_load = lax.all_to_all(send_load, "elem", split_axis=0, concat_axis=0, tiled=True)
    answers = lax.all_to_all(
        evaluate_rows(recv_rows, recv_load), "elem", split_axis=0, concat_axis=0, tiled=True
    )
    combined = jnp.where(is_home[:, None], home_combined, answers[owner_flat, slot_index])
    interp = combined[:, :tracers].reshape(shape4)
    lowest = combined[:, tracers : 2 * tracers].reshape(shape4)
    highest = combined[:, 2 * tracers :].reshape(shape4)
    clipped, upper, lower, sums = fixer_terms(interp, lowest, highest, mass_new)
    source_total, clip_total, up_total, down_total = lax.psum(
        (local_source, sums[0], sums[1], sums[2]), "elem"
    )
    result = apply_fix(clipped, upper, lower, source_total, clip_total, up_total, down_total)
    return result.reshape(elems, levels, width)


def solution(mesh):
    placed = (
        P("elem", None, None),
        P("elem", None),
        P("elem", None),
        P("elem", None, None),
        P("elem", None),
        P(None, "elem", None),
    )
    return jax.shard_map(
        body, mesh=mesh, in_specs=placed, out_specs=P("elem", None, None), check_vma=False
    )
```

profile of v0, /device:TPU:0, one launch (start us, length us, event | category | flops | bytes accessed | tf_op | source)
XLA Modules:
  0.0 119.2 jit_solution(8861033583044019252)
XLA Ops:
  0.0 0.7 compare_not_fusion
  0.7 0.7 fusion.18
  1.4 9.0 %reduce-window.6 = s32[32,8,128]{2,1,0:T(8,128)S(1)} reduce-window(s32[32,8,128]{2,1,0:T(8,128)S(1)} %fusion.18, s32[]{:T(128)} %copy.77), window={size=1x1x128 pad=0_0x0_0x127_0}, to_apply=%region_4.5 | reduce-window | flops 4161536 | bytes 262148 | tf_op jit(solution)/shard_map/reduce-window
  10.9 0.7 fusion.25
  11.6 0.7 fusion.15
  12.3 0.7 fusion.21
  13.1 0.7 multiply_reduce_fusion.4
  13.8 0.7 broadcast_multiply_fusion.4
  14.5 4.3 %scatter_custom_fusion = s32[1024]{0:T(1024)S(1)} fusion(s32[1024]{0:T(1024)S(1)} %broadcast_select_fusion, s32[1024]{0:T(1024)S(1)} %get-tuple-element.216, s32[]{:T(128)} %copy.77), kind=kCustom, calls=%fused_computation.82 | custom fusion | bytes 4100
  18.8 0.7 all_to_all.12
  19.5 7.3 %all-to-all-start = ((s32[32,1,32]{2,1,0:T(1,128)}), s32[32,1,32]{2,1,0:T(1,128)S(1)}, u32[]{:S(2)}, u32[]{:S(2)}) async-start(s32[32,1,32]{2,1,0:T(1,128)} %all_to_all.12), calls=%async_computation | async-start | bytes 32768 | tf_op jit(solution)/shard_map/all_to_all | solution.py:130
  26.8 0.7 fusion.27
  27.5 1.3 %reshape.520 = f32[64,16,40]{2,1,0:T(8,128)S(1)} reshape(f32[8,8,640]{2,1,0:T(8,128)} %param.10) | data formatting | bytes 327680 | tf_op jit(solution)/shard_map/reshape | solution.py:94
  29.2 0.2 copy.44
  29.4 3.2 %scatter_custom_fusion.1 = f32[1024,2]{1,0:T(8,128)S(1)} fusion(s32[1024]{0:T(1024)S(1)} %broadcast_select_fusion, f32[1024,2]{1,0:T(8,128)S(1)} %copy.44, f32[]{:T(128)} %constant.133.clone.1), kind=kCustom, calls=%fused_computation.31 | custom fusion | bytes 8196
  32.7 0.9 copy.45
  33.5 0.4 all-to-all-done
  34.0 5.4 %all-to-all-start.1 = ((f32[32,32,2]{1,2,0:T(2,128)}), f32[32,32,2]{1,2,0:T(2,128)S(1)}, u32[]{:S(2)}, u32[]{:S(2)}) async-start(f32[32,32,2]{1,2,0:T(2,128)} %copy.45), calls=%async_computation.1 | async-start | bytes 65536 | tf_op jit(solution)/shard_map/all_to_all | solution.py:131
  39.5 0.4 reshape.519
  39.9 0.6 broadcast.868
  40.5 0.7 reduce.11
  41.3 5.3 %all-to-all-done.1 = f32[32,32,2]{1,2,0:T(2,128)S(1)} async-done(((f32[32,32,2]{1,2,0:T(2,128)}), f32[32,32,2]{1,2,0:T(2,128)S(1)}, u32[]{:S(2)}, u32[]{:S(2)}) %all-to-all-start.1) | async-done | bytes 8224 | tf_op jit(solution)/shard_map/all_to_all | solution.py:131
  47.0 4.4 %while.23 = (s32[]{:T(128)}, f32[2,512,120]{1,2,0:T(8,128)S(1)}, s32[2,512]{1,0:T(2,128)S(1)}, f32[2,512,16]{1,0,2:T(2,128)S(1)}, f32[1024,40]{1,0:T(8,128)S(1)}, /*index=5*/f32[64,80]{1,0:T(8,128)S(1)}, s32[]{:T(128)}) while((s32[]{:T(128)}, f32[2,512,120]{1,2,0:T(8,128)S(1)}, s32[2,512]{1,0:T(2,128)S(1)}, ...), condition=%wide.region_10.11_spmd.clone, body=%wide.region_9.10_spmd.clone.sunk | while | flops 283799552 | bytes 5550169 | solution.py:120
  47.1 0.3 broadcast_multiply_fusion.8
  47.4 1.5 %fusion.62 = f32[512,40]{0,1:T(8,128)S(1)} fusion(f32[512,1024]{0,1:T(8,128)S(1)} %bitcast.94, f32[1024,40]{1,0:T(8,128)S(1)} %get-tuple-element.316), kind=kOutput, calls=%fused_computation.114.clone.1 | convolution fusion | flops 251658240 | bytes 2342912 | tf_op jit(solution)/shard_map/while/body/eval_jaxpr/dot_general | solution.py:116
  48.9 0.3 fusion.60
  49.3 0.3 broadcast_multiply_fusion.8
  49.6 1.5 %fusion.62 = f32[512,40]{0,1:T(8,128)S(1)} fusion(f32[512,1024]{0,1:T(8,128)S(1)} %bitcast.94, f32[1024,40]{1,0:T(8,128)S(1)} %get-tuple-element.316), kind=kOutput, calls=%fused_computation.114.clone.1 | convolution fusion | flops 251658240 | bytes 2342912 | tf_op jit(solution)/shard_map/while/body/eval_jaxpr/dot_general | solution.py:116
  51.1 0.3 fusion.60
  51.4 1.0 copy.48
  52.4 2.6 %all-to-all-start.2 = ((f32[32,32,120]{2,1,0:T(8,128)}), f32[32,32,120]{2,1,0:T(8,128)S(1)}, u32[]{:S(2)}, u32[]{:S(2)}) async-start(f32[32,32,120]{2,1,0:T(8,128)} %bitcast.12), calls=%async_computation.2 | async-start | bytes 1048576 | tf_op jit(solution)/shard_map/all_to_all | solution.py:132
  55.1 4.4 %while.22 = (s32[]{:T(128)}, f32[2,512,120]{1,2,0:T(8,128)S(1)}, s32[2,512]{1,0:T(2,128)S(1)}, f32[2,512,16]{1,0,2:T(2,128)S(1)}, f32[1024,40]{1,0:T(8,128)S(1)}, /*index=5*/f32[64,80]{1,0:T(8,128)S(1)}, s32[]{:T(128)}) while((s32[]{:T(128)}, f32[2,512,120]{1,2,0:T(8,128)S(1)}, s32[2,512]{1,0:T(2,128)S(1)}, ...), condition=%wide.region_3.4_spmd.clone, body=%wide.region_2.3_spmd.clone.sunk | while | flops 283799552 | bytes 5550169 | solution.py:120
  55.2 0.3 broadcast_multiply_fusion.7
  55.5 1.5 %fusion.55 = f32[512,40]{0,1:T(8,128)S(1)} fusion(f32[512,1024]{0,1:T(8,128)S(1)} %bitcast.95, f32[1024,40]{1,0:T(8,128)S(1)} %get-tuple-element.337), kind=kOutput, calls=%fused_computation.113.clone.1 | convolution fusion | flops 251658240 | bytes 2342912 | tf_op jit(solution)/shard_map/while/body/eval_jaxpr/dot_general | solution.py:116
  57.0 0.3 fusion.53
  57.4 0.3 broadcast_multiply_fusion.7
  57.7 1.5 %fusion.55 = f32[512,40]{0,1:T(8,128)S(1)} fusion(f32[512,1024]{0,1:T(8,128)S(1)} %bitcast.95, f32[1024,40]{1,0:T(8,128)S(1)} %get-tuple-element.337), kind=kOutput, calls=%fused_computation.113.clone.1 | convolution fusion | flops 251658240 | bytes 2342912 | tf_op jit(solution)/shard_map/while/body/eval_jaxpr/dot_general | solution.py:116
  59.2 0.3 fusion.53
  60.1 0.3 mul.428
  60.5 10.1 %all-to-all-done.2 = f32[32,32,120]{2,1,0:T(8,128)S(1)} async-done(((f32[32,32,120]{2,1,0:T(8,128)}), f32[32,32,120]{2,1,0:T(8,128)S(1)}, u32[]{:S(2)}, u32[]{:S(2)}) %all-to-all-start.2) | async-done | bytes 491552 | tf_op jit(solution)/shard_map/all_to_all | solution.py:132
  70.6 6.8 %gather_fusion = f32[1024,120]{1,0:T(8,128)S(1)} fusion(f32[32,32,120]{2,1,0:T(8,128)S(1)} %all-to-all-done.2, s32[1024]{0:T(1024)S(1)} %bitcast.96), kind=kCustom, calls=%fused_computation | custom fusion | bytes 991232 | tf_op jit(solution)/shard_map/gather | solution.py:135
  77.6 0.3 fusion.26
  77.9 0.3 reshape.526
  78.1 0.3 reshape.527
  78.4 0.3 reshape.528
  78.6 0.4 multiply_reduce_fusion.1
  79.0 39.2 %all-reduce = (f32[8,40]{1,0:T(8,128)S(1)}, f32[8,40]{1,0:T(8,128)S(1)}, f32[8,40]{1,0:T(8,128)S(1)}, f32[8,40]{1,0:T(8,128)S(1)}) all-reduce(f32[8,40]{1,0:T(8,128)S(1)} %get-tuple-element.158, f32[8,40]{1,0:T(8,128)S(1)} %reduce_sum.58, f32[8,40]{1,0:T(8,128)S(1)} %get-tuple-element.159, ...), channel_id=1, replica_groups=mesh['elem'=32] {'elem'}, use_global_device_ids=true, to_apply=%region_19.20 | all-reduce | flops 1280 | bytes 10240 | tf_op jit(solution)/shard_map/psum | solution.py:140
  118.5 0.7 multiply_add_fusion.1
  (68 shorter events, 2.9 us)
Async XLA Ops:
  10.5 29.0 %copy-start = (f32[8,8,640]{2,1,0:T(8,128)S(1)}, f32[8,8,640]{2,1,0:T(8,128)}, u32[]{:S(2)}) copy-start(f32[8,8,640]{2,1,0:T(8,128)} %param.10) | copy-start | bytes 491524
  19.5 14.4 %all-to-all-start = ((s32[32,1,32]{2,1,0:T(1,128)}), s32[32,1,32]{2,1,0:T(1,128)S(1)}, u32[]{:S(2)}, u32[]{:S(2)}) async-start(s32[32,1,32]{2,1,0:T(1,128)} %all_to_all.12), calls=%async_computation | async-start | bytes 32768 | tf_op jit(solution)/shard_map/all_to_all | solution.py:130
  34.0 12.7 %all-to-all-start.1 = ((f32[32,32,2]{1,2,0:T(2,128)}), f32[32,32,2]{1,2,0:T(2,128)S(1)}, u32[]{:S(2)}, u32[]{:S(2)}) async-start(f32[32,32,2]{1,2,0:T(2,128)} %copy.45), calls=%async_computation.1 | async-start | bytes 65536 | tf_op jit(solution)/shard_map/all_to_all | solution.py:131
  52.4 18.2 %all-to-all-start.2 = ((f32[32,32,120]{2,1,0:T(8,128)}), f32[32,32,120]{2,1,0:T(8,128)S(1)}, u32[]{:S(2)}, u32[]{:S(2)}) async-start(f32[32,32,120]{2,1,0:T(8,128)} %bitcast.12), calls=%async_computation.2 | async-start | bytes 1048576 | tf_op jit(solution)/shard_map/all_to_all | solution.py:132
  55.1 4.6 %copy-start.1 = (f32[8,128]{1,0:T(8,128)S(1)}, f32[8,128]{1,0:T(8,128)}, u32[]{:S(2)}) copy-start(f32[8,128]{1,0:T(8,128)} %param.12) | copy-start | bytes 12292
  55.1 4.7 %copy-start.2 = (f32[8,128]{1,0:T(8,128)S(1)}, f32[8,128]{1,0:T(8,128)}, u32[]{:S(2)}) copy-start(f32[8,128]{1,0:T(8,128)} %param.11) | copy-start | bytes 12292
where the time goes:
time: 120 us; the launch traced here: 119 us
  blocking collectives  39.2 us (33%)
  local copies, waits for them, and re-layouts  23.1 us (19%)
  other arithmetic  18 us (15%)
  waiting for transfers between devices  15.8 us (13%)
  starting transfers between devices  15.3 us (13%)
  matrix products  7.11 us (6%)
    psum x1, blocking collectives, body(): lax.psum((local_source, sums[0], sums[1], sums[2]), 'elem')  39.2 us
    all_to_all x1, waiting for transfers between devices, body(): lax.all_to_all(evaluate_rows(recv_rows, recv_load), 'elem', split_axis=0,...  10.1 us
    another operation x2, other arithmetic  9.04 us
    unnamed x8, local copies, waits for them, and re-layouts  7.54 us
    all_to_all x1, starting transfers between devices, body(): lax.all_to_all(send_rows, 'elem', split_axis=0, concat_axis=0, tiled=True)  7.3 us
    gather x1, local copies, waits for them, and re-layouts, body(): answers[owner_flat, slot_index]  6.78 us
    dot_general x4, matrix products, one_block(): values = jnp.dot(spread, node_table, precision=lax.Precision.HIGHEST)  6.02 us
    all_to_all x1, starting transfers between devices, body(): lax.all_to_all(send_load, 'elem', split_axis=0, concat_axis=0, tiled=True)  5.42 us
  transfers between devices with their start and end apart: 3, of which 3 were waited for; matrix products, arithmetic and copies ran while one was open for 12% of the time, Pallas kernels for 0%

commit v1 on v0

v1 whole, which is shorter than its diff:
```python
import functools

import jax
import jax.numpy as jnp
from jax import lax
from jax.experimental import pallas as pl
from jax.experimental.pallas import tpu as pltpu
from jax.sharding import PartitionSpec as P

GLL_NODES = (-1.0, -0.4472135954999579, 0.4472135954999579, 1.0)
NODES = 16
MESH = pl.DeviceIdType.MESH
F32 = jnp.float32
BF16 = jnp.bfloat16
HIGHEST = lax.Precision.HIGHEST


def one_axis(coord):
    away = [coord - node for node in GLL_NODES]
    columns = []
    for own in range(4):
        factor, scale = None, 1.0
        for other in range(4):
            if other != own:
                factor = away[other] if factor is None else factor * away[other]
                scale *= GLL_NODES[own] - GLL_NODES[other]
        columns.append(factor * (1.0 / scale))
    return columns


def split3(x):
    high = x.astype(BF16).astype(F32)
    rest = x - high
    middle = rest.astype(BF16).astype(F32)
    return high, middle, rest - middle


def iota(shape, axis):
    return lax.broadcasted_iota(jnp.int32, shape, axis)


def dot_nt(a, b, precision=None):
    return lax.dot_general(
        a, b, (((1,), (1,)), ((), ())), precision=precision, preferred_element_type=F32
    )


def dot_tn(a, b, precision=None):
    return lax.dot_general(
        a, b, (((0,), (0,)), ((), ())), precision=precision, preferred_element_type=F32
    )


def kernel(
    devices, cap,
    tracer, old_mass, new_mass, owner, local, coord, out,
    table, home_c, home_u, home_l, far_c, far_u, far_l, spread, la_home, la_far, fields,
    req_out, req_in, sum_out, sum_in, ans_out, ans_in, turned,
    req_send, req_recv, sum_send, sum_recv, ans_send, ans_recv,
):
    elems, levels, width = tracer.shape
    tracers = width // NODES
    points = levels * NODES
    cells = elems * levels
    group = points // cap
    blocks = devices // group
    me = lax.axis_index("elem")

    def peer(step):
        return lax.rem(me + step, devices)

    barrier = pltpu.get_barrier_semaphore()

    @pl.loop(1, devices)
    def _(step):
        pl.semaphore_signal(barrier, inc=1, device_id=(peer(step),), device_id_type=MESH)

    own = owner[...]
    away_ids = iota((devices, points), 0)
    away_ids = jnp.where(away_ids == me, -1, away_ids)
    hot = [(own[e : e + 1, :] == away_ids).astype(F32) for e in range(elems)]
    row, column = iota((points, 2 * points), 0), iota((points, 2 * points), 1)
    ladder = ((row <= column) | (column >= points)).astype(BF16)
    counted = jnp.dot(jnp.concatenate(hot, axis=0).astype(BF16), ladder, preferred_element_type=F32)
    before = jnp.zeros((devices, points), F32)
    base = (away_ids * cap).astype(F32)
    ranks, slots = [], []
    for e in range(elems):
        part = counted[e * devices : (e + 1) * devices]
        rank = jnp.sum(hot[e] * (part[:, :points] + before), axis=0, keepdims=True) - 1.0
        ranks.append(rank)
        slots.append(jnp.sum(hot[e] * base, axis=0, keepdims=True) + rank)
        before = before + part[:, points:]

    level_of = lax.div(iota((elems, points), 1), NODES)
    cell_home = (local[...] * levels + level_of).astype(F32)
    payload = [split3(x) for x in (cell_home, coord[0], coord[1], new_mass[...])]
    place = iota((cap, points), 0).astype(F32)
    chosen = []
    for term in range(3):
        lanes = []
        for e in range(elems):
            mine = place == ranks[e]
            lanes.append(
                jnp.concatenate(
                    [jnp.where(mine, f[term][e : e + 1, :], 0.0) for f in payload], axis=0
                ).astype(BF16)
            )
        chosen.append(jnp.concatenate(lanes, axis=1))
    hots = jnp.concatenate([h.astype(BF16) for h in hot], axis=1)
    asked = dot_nt(hots, chosen[0]) + dot_nt(hots, chosen[1]) + dot_nt(hots, chosen[2])
    req_out[...] = asked.reshape(devices, 1, points)
    req_in[pl.ds(me, 1)] = jnp.zeros((1, 1, points), F32)

    pl.semaphore_wait(barrier, devices - 1)

    def request(to, source):
        return pltpu.make_async_remote_copy(
            src_ref=req_out.at[to], dst_ref=req_in.at[source],
            send_sem=req_send.at[to], recv_sem=req_recv.at[source],
            device_id=(to,), device_id_type=MESH,
        )

    @pl.loop(1, devices)
    def _(step):
        request(peer(step), me).start()

    flat = tracer[...].reshape(cells, width)
    table[...] = jnp.concatenate(split3(flat), axis=0).T.astype(BF16)

    point = iota((levels, points), 1)
    at_level = lax.div(point, NODES) == iota((levels, points), 0)
    masses = jnp.concatenate(
        [jnp.where(at_level, old_mass[e : e + 1, :], 0.0) for e in range(elems)], axis=0
    )
    widen = (
        lax.rem(iota((points, width), 0), NODES) == lax.div(iota((points, width), 1), tracers)
    ).astype(BF16)
    wide = jnp.zeros((cells, width), F32)
    for term in split3(masses):
        wide = wide + jnp.dot(term.astype(BF16), widen, preferred_element_type=F32)
    held = wide * flat
    by_node = held[:levels]
    for e in range(1, elems):
        by_node = by_node + held[e * levels : (e + 1) * levels]
    narrow = (lax.rem(iota((width, points), 0), tracers) == iota((width, points), 1)).astype(F32)
    source = jnp.dot(by_node, narrow, precision=HIGHEST, preferred_element_type=F32)

    cell_ids = lax.rem(iota((3 * cells, points), 0), cells).astype(F32)

    def evaluate(cell, wa, wb):
        chosen = (cell_ids == cell).astype(BF16)
        values = jnp.dot(table[...], chosen, preferred_element_type=F32)
        interp = lowest = highest = None
        for k in range(NODES):
            value = values[k * tracers : (k + 1) * tracers]
            term = (wa[k // 4] * wb[k % 4]) * value
            interp = term if k == 0 else interp + term
            lowest = value if k == 0 else jnp.minimum(lowest, value)
            highest = value if k == 0 else jnp.maximum(highest, value)
        clipped = jnp.minimum(jnp.maximum(interp, lowest), highest)
        margin = 0.01 + 0.05 * (highest - lowest)
        return clipped, highest + margin - clipped, clipped - lowest + margin

    def mass_sums(weights, clipped, upper, lower):
        rest = jnp.zeros((points - 3 * tracers, points), F32)
        terms = jnp.concatenate([-clipped, upper, lower, rest], axis=0)
        return dot_nt(weights, terms, HIGHEST)

    for i, value in enumerate(one_axis(coord[0]) + one_axis(coord[1])):
        la_home[i] = value.reshape(elems, 1, points)
    fields[pl.ds(0, elems)] = cell_home.reshape(elems, 1, points)
    fields[pl.ds(elems, elems)] = jnp.where(own == me, new_mass[...], 0.0).reshape(
        elems, 1, points
    )

    def home_block(e, sums):
        results = evaluate(
            fields[e], [la_home[i, e] for i in range(4)], [la_home[4 + i, e] for i in range(4)]
        )
        home_c[e], home_u[e], home_l[e] = results
        weights = jnp.where(at_level, fields[elems + e], 0.0)
        return sums + mass_sums(weights, *results)

    sums = lax.fori_loop(0, elems, home_block, source)

    slot_ids = iota((devices * cap, points), 0).astype(F32)
    for e in range(elems):
        spread[:, e * points : (e + 1) * points] = (slot_ids == slots[e]).astype(BF16)

    @pl.loop(1, devices)
    def _(step):
        request(peer(step), peer(step)).wait_recv()

    got = req_in[...].reshape(devices, points)
    r, c = iota((devices, points), 0), lax.div(iota((devices, points), 1), cap)
    bit = 1
    while bit < group:
        down = pltpu.roll(pltpu.roll(got, bit, 0), points - cap * bit, 1)
        up = pltpu.roll(pltpu.roll(got, devices - bit, 0), cap * bit, 1)
        row_bit, lane_bit = (r & bit) != 0, (c & bit) != 0
        got = jnp.where(row_bit == lane_bit, got, jnp.where(row_bit, down, up))
        bit *= 2
    la_far[4] = got.reshape(devices, 1, points)
    for i, value in enumerate(one_axis(got)):
        la_far[i] = value.reshape(devices, 1, points)

    level_ids = iota((levels, points), 0).astype(F32)

    def slot_level(b):
        cell = la_far[4, group * b]
        return cell, level_ids == cell - levels * jnp.floor((cell + 0.5) / levels)

    def far_block(b, sums):
        first = group * b
        cell, here = slot_level(b)
        results = evaluate(
            cell,
            [la_far[i, first + 1] for i in range(4)],
            [la_far[i, first + 2] for i in range(4)],
        )
        far_c[b], far_u[b], far_l[b] = results
        return sums + mass_sums(jnp.where(here, la_far[4, first + 3], 0.0), *results)

    sums = lax.fori_loop(0, blocks, far_block, sums)

    sum_out[...] = sums
    sum_in[pl.ds(me, 1)] = sums.reshape(1, levels, points)

    def share(to, source):
        return pltpu.make_async_remote_copy(
            src_ref=sum_out, dst_ref=sum_in.at[source],
            send_sem=sum_send.at[to], recv_sem=sum_recv.at[source],
            device_id=(to,), device_id_type=MESH,
        )

    @pl.loop(1, devices)
    def _(step):
        share(peer(step), me).start()

    @pl.loop(1, devices)
    def _(step):
        share(peer(step), peer(step)).wait_recv()

    total = jnp.sum(sum_in[...], axis=0)
    lane = iota((levels, points), 1)
    up_total = pltpu.roll(total, points - tracers, 1)
    down_total = pltpu.roll(total, points - 2 * tracers, 1)
    inside = lane < tracers
    plus = jnp.where(inside, jnp.maximum(total, 0.0) / jnp.where(inside, up_total, 1.0), 0.0)
    minus = jnp.where(inside, jnp.minimum(total, 0.0) / jnp.where(inside, down_total, 1.0), 0.0)
    factors = plus + pltpu.roll(minus, tracers, 1)

    def fix(here, clipped, upper, lower):
        by_lane = dot_tn(factors, here.astype(F32), HIGHEST)
        return clipped + by_lane[:tracers] * upper + by_lane[tracers : 2 * tracers] * lower

    def answer(to, source):
        return pltpu.make_async_remote_copy(
            src_ref=ans_out.at[to], dst_ref=ans_in.at[source],
            send_sem=ans_send.at[to], recv_sem=ans_recv.at[source],
            device_id=(to,), device_id_type=MESH,
        )

    lane_block = lax.div(iota((8, points), 1), cap)

    def swap_blocks(tiles):
        bit = 1
        while bit < group:
            moved = list(tiles)
            for t in range(group):
                if t & bit == 0:
                    odd = (lane_block & bit) != 0
                    a, b = tiles[t], tiles[t + bit]
                    moved[t] = jnp.where(odd, pltpu.roll(b, cap * bit, 1), a)
                    moved[t + bit] = jnp.where(odd, b, pltpu.roll(a, points - cap * bit, 1))
            tiles = moved
            bit *= 2
        return tiles

    my_place = lax.rem(me, group)

    def send_block(turn, carry):
        b = lax.rem(turn + lax.div(me, group), blocks)
        _, here = slot_level(b)
        fixed = fix(here, far_c[b], far_u[b], far_l[b])
        tiles = swap_blocks([fixed[8 * t : 8 * t + 8] for t in range(group)])
        last = fixed[8 * group :]
        for i in range(group):
            to = group * b + i
            ans_out[to, 0:8] = tiles[i]
            ans_out[to, 8:16] = pltpu.roll(last, lax.rem(my_place + group - i, group) * cap, 1)

            @pl.when(to != me)
            def _():
                answer(to, me).start()

        return carry

    lax.fori_loop(0, blocks, send_block, 0)

    def home_fix(e, carry):
        home_c[e] = fix(at_level, home_c[e], home_u[e], home_l[e])
        return carry

    lax.fori_loop(0, elems, home_fix, 0)
    ans_in[pl.ds(me, 1)] = jnp.zeros((1, 16, points), F32)

    @pl.loop(1, devices)
    def _(step):
        answer(peer(step), peer(step)).wait_recv()

    columns = []
    for b in range(blocks):
        tiles = swap_blocks([ans_in[group * b + i, 0:8] for i in range(group)])
        last = ans_in[group * b, 8:16]
        for i in range(1, group):
            last = jnp.where(lane_block == i, ans_in[group * b + i, 8:16], last)
        columns.append(jnp.concatenate(tiles + [last], axis=0))
    answers = jnp.concatenate(columns, axis=1)
    terms = jnp.concatenate(split3(answers), axis=0).astype(BF16)
    landed = jnp.dot(terms, spread[...], preferred_element_type=F32)
    landed = landed[:tracers] + landed[tracers : 2 * tracers] + landed[2 * tracers :]

    pad = jnp.zeros((points - tracers, points), F32)
    for e in range(elems):
        mixed = jnp.where(own[e : e + 1] == me, home_c[e], landed[:, e * points : (e + 1) * points])
        turned[e] = jnp.concatenate([mixed, pad], axis=0).T
        for k in range(NODES):
            out[e, :, k * tracers : (k + 1) * tracers] = turned[
                e, pl.ds(k, levels, stride=NODES), :
            ][:, :tracers]

    @pl.loop(1, devices)
    def _(step):
        to = peer(step)
        request(to, me).wait_send()
        share(to, me).wait_send()
        answer(to, me).wait_send()


def body(tracer, old_mass, new_mass, dep_owner, dep_local, dep_coord):
    devices = lax.axis_size("elem")
    elems, levels, width = tracer.shape
    tracers = width // NODES
    points = levels * NODES
    cap = elems * points // 32
    blocks = devices * cap // points
    cells = elems * levels
    vmem = pltpu.VMEM
    dma = pltpu.SemaphoreType.DMA
    return pl.pallas_call(
        functools.partial(kernel, devices, cap),
        out_shape=jax.ShapeDtypeStruct(tracer.shape, F32),
        in_specs=[pl.BlockSpec(memory_space=vmem)] * 6,
        out_specs=pl.BlockSpec(memory_space=vmem),
        scratch_shapes=[
            vmem((width, 3 * cells), BF16),
            *[vmem((elems, tracers, points), F32)] * 3,
            *[vmem((blocks, tracers, points), F32)] * 3,
            vmem((devices * cap, elems * points), BF16),
            vmem((8, elems, 1, points), F32),
            vmem((5, devices, 1, points), F32),
            vmem((2 * elems, 1, points), F32),
            vmem((devices, 1, points), F32),
            vmem((devices, 1, points), F32),
            vmem((levels, points), F32),
            vmem((devices, levels, points), F32),
            vmem((devices, 16, points), F32),
            vmem((devices, 16, points), F32),
            vmem((elems, points, points), F32),
            *[dma((devices,))] * 6,
        ],
        compiler_params=pltpu.CompilerParams(
            collective_id=0, has_side_effects=True, vmem_limit_bytes=48 * 1024 * 1024
        ),
    )(
        tracer, old_mass, new_mass,
        dep_owner.reshape(elems, points), dep_local, dep_coord,
    )


def solution(mesh):
    placed = (
        P("elem", None, None),
        P("elem", None),
        P("elem", None),
        P("elem", None, None),
        P("elem", None),
        P(None, "elem", None),
    )
    return jax.shard_map(
        body, mesh=mesh, in_specs=placed, out_specs=P("elem", None, None), check_vma=False
    )
```

time: 120 us -> 40.5 us (0.34)
  blocking collectives: 39.2 us -> 0 us
  Pallas kernels: 0 us -> 35.1 us
  local copies, waits for them, and re-layouts: 23.1 us -> 5.03 us
  other arithmetic: 18 us -> 0 us
  waiting for transfers between devices: 15.8 us -> 0 us
  starting transfers between devices: 15.3 us -> 0 us
  matrix products: 7.11 us -> 0 us
    psum x1 -> x0, blocking collectives: 39.2 us -> none  [body(): lax.psum((local_source, sums[0], sums[1], sums[2]), 'elem')]
    pallas_call x0 -> x1, Pallas kernels: none -> 35.1 us  [body(): pl.pallas_call(functools.partial(kernel, devices, cap), out_shape=jax.Sha...]
    all_to_all x3 -> x0, waiting for transfers between devices: 15.8 us -> none  [the longest x1 10.1 us: body(): lax.all_to_all(evaluate_rows(recv_rows, recv_load), 'elem', split_axis=0,...]
    all_to_all x3 -> x0, starting transfers between devices: 15.3 us -> none  [the longest x1 7.3 us: body(): lax.all_to_all(send_rows, 'elem', split_axis=0, concat_axis=0, tiled=True)]
    another operation x5 -> x0, other arithmetic: 9.13 us -> none
    dot_general x8 -> x0, matrix products: 7.11 us -> none  [the longest x4 6.02 us: one_block(): values = jnp.dot(spread, node_table, precision=lax.Precision.HIGHEST)]
    gather x1 -> x0, local copies, waits for them, and re-layouts: 6.78 us -> none  [body(): answers[owner_flat, slot_index]]
    unnamed x8 -> x13, local copies, waits for them, and re-layouts: 7.54 us -> 5.03 us
  transfers between devices with their start and end apart: 3 -> 0, of which waited for: 3 -> 0; matrix products, arithmetic and copies ran while one was open for 12% -> 0% of each run, Pallas kernels for 0% -> 0%
where the time goes in v1:
time: 40.5 us; the launch traced here: 40.2 us
  Pallas kernels  35.1 us (87%)
  local copies, waits for them, and re-layouts  5.03 us (12%)
    pallas_call x1, Pallas kernels, body(): pl.pallas_call(functools.partial(kernel, devices, cap), out_shape=jax.Sha...  35.1 us
    unnamed x13, local copies, waits for them, and re-layouts  5.03 us

profile of v1, /device:TPU:0, one launch (start us, length us, event | category | flops | bytes accessed | tf_op | source)
XLA Modules:
  0.0 40.2 jit_solution(7680285707471091564)
XLA Ops:
  0.0 0.0 copy-start
  0.0 0.9 %copy-done = f32[8,8,640]{2,1,0:T(8,128)S(1)} copy-done((f32[8,8,640]{2,1,0:T(8,128)S(1)}, f32[8,8,640]{2,1,0:T(8,128)}, u32[]{:S(2)}) %copy-start) | copy-done | bytes 163864
  0.9 0.0 copy-start.1
  0.9 0.7 %copy-done.1 = f32[2,8,128]{2,1,0:T(8,128)S(1)} copy-done((f32[2,8,128]{2,1,0:T(8,128)S(1)}, f32[2,8,128]{2,1,0:T(8,128)}, u32[]{:S(2)}) %copy-start.1) | copy-done | bytes 8216
  1.6 0.0 copy-start.2
  1.6 0.7 %copy-done.2 = f32[8,128]{1,0:T(8,128)S(1)} copy-done((f32[8,128]{1,0:T(8,128)S(1)}, f32[8,128]{1,0:T(8,128)}, u32[]{:S(2)}) %copy-start.2) | copy-done | bytes 4120
  2.3 0.0 copy-start.3
  2.3 0.7 %copy-done.3 = f32[8,128]{1,0:T(8,128)S(1)} copy-done((f32[8,128]{1,0:T(8,128)S(1)}, f32[8,128]{1,0:T(8,128)}, u32[]{:S(2)}) %copy-start.3) | copy-done | bytes 4120
  3.0 0.0 copy-start.4
  3.0 0.7 %copy-done.4 = s32[8,128,1]{1,2,0:T(1,128)S(1)} copy-done((s32[8,128,1]{1,2,0:T(1,128)S(1)}, s32[8,128,1]{1,2,0:T(1,128)}, u32[]{:S(2)}) %copy-start.4) | copy-done | bytes 4120
  3.7 0.0 copy-start.5
  3.7 0.7 %copy-done.5 = s32[8,128]{1,0:T(8,128)S(1)} copy-done((s32[8,128]{1,0:T(8,128)S(1)}, s32[8,128]{1,0:T(8,128)}, u32[]{:S(2)}) %copy-start.5) | copy-done | bytes 4120
  4.4 35.1 %shard_map.64 = f32[8,8,640]{2,1,0:T(8,128)S(1)} custom-call(f32[8,8,640]{2,1,0:T(8,128)S(1)} %copy-done, f32[8,128]{1,0:T(8,128)S(1)} %copy-done.2, f32[8,128]{1,0:T(8,128)S(1)} %copy-done.3, s32[8,128]{1,0:T(8,128)S(1)} %bitcast.1, s32[8,128]{1,0:T(8,128)S(1)} %copy-done.5, f32[2,8,128]{2,1,0:T(8,128)S(1)} %copy-done.1), custom_call_target="tpu_custom_call" | custom-call | tf_op jit(solution)/shard_map/pallas_call | solution.py:352
  39.5 0.7 %copy.8 = f32[8,8,640]{2,1,0:T(8,128)} copy(f32[8,8,640]{2,1,0:T(8,128)S(1)} %shard_map.64) | data formatting | bytes 327680
Async XLA Ops:
  0.0 0.9 %copy-start = (f32[8,8,640]{2,1,0:T(8,128)S(1)}, f32[8,8,640]{2,1,0:T(8,128)}, u32[]{:S(2)}) copy-start(f32[8,8,640]{2,1,0:T(8,128)} %tracer.1) | copy-start | bytes 491524
  0.9 0.7 %copy-start.1 = (f32[2,8,128]{2,1,0:T(8,128)S(1)}, f32[2,8,128]{2,1,0:T(8,128)}, u32[]{:S(2)}) copy-start(f32[2,8,128]{2,1,0:T(8,128)} %coord.1) | copy-start | bytes 24580
  1.6 0.7 %copy-start.2 = (f32[8,128]{1,0:T(8,128)S(1)}, f32[8,128]{1,0:T(8,128)}, u32[]{:S(2)}) copy-start(f32[8,128]{1,0:T(8,128)} %old_mass.1) | copy-start | bytes 12292
  2.3 0.7 %copy-start.3 = (f32[8,128]{1,0:T(8,128)S(1)}, f32[8,128]{1,0:T(8,128)}, u32[]{:S(2)}) copy-start(f32[8,128]{1,0:T(8,128)} %new_mass.1) | copy-start | bytes 12292
  3.0 0.7 %copy-start.4 = (s32[8,128,1]{1,2,0:T(1,128)S(1)}, s32[8,128,1]{1,2,0:T(1,128)}, u32[]{:S(2)}) copy-start(s32[8,128,1]{1,2,0:T(1,128)} %param.9) | copy-start | bytes 12292
  3.7 0.7 %copy-start.5 = (s32[8,128]{1,0:T(8,128)S(1)}, s32[8,128]{1,0:T(8,128)}, u32[]{:S(2)}) copy-start(s32[8,128]{1,0:T(8,128)} %local.1) | copy-start | bytes 12292

commit v2 on v1

--- a/solution.py
+++ b/solution.py
@@ -53,7 +53,8 @@
 
 def kernel(
     devices, cap,
-    tracer, old_mass, new_mass, owner, local, coord, out,
+    tracer_in, old_in, new_in, owner_in, local_in, coord_in, out,
+    tracer, old_mass, new_mass, owner, local, coord, load,
     table, home_c, home_u, home_l, far_c, far_u, far_l, spread, la_home, la_far, fields,
     req_out, req_in, sum_out, sum_in, ans_out, ans_in, turned,
     req_send, req_recv, sum_send, sum_recv, ans_send, ans_recv,
@@ -69,11 +70,30 @@
     def peer(step):
         return lax.rem(me + step, devices)
 
+    loads = [
+        pltpu.make_async_copy(source, target, load.at[i])
+        for i, (source, target) in enumerate(
+            (
+                (owner_in, owner),
+                (local_in, local),
+                (coord_in, coord),
+                (new_in, new_mass),
+                (old_in, old_mass),
+                (tracer_in, tracer),
+            )
+        )
+    ]
+    for copy in loads:
+        copy.start()
+
     barrier = pltpu.get_barrier_semaphore()
 
     @pl.loop(1, devices)
     def _(step):
         pl.semaphore_signal(barrier, inc=1, device_id=(peer(step),), device_id_type=MESH)
+
+    for copy in loads[:4]:
+        copy.wait()
 
     own = owner[...]
     away_ids = iota((devices, points), 0)
@@ -125,6 +145,9 @@
     def _(step):
         request(peer(step), me).start()
 
+    for copy in loads[4:]:
+        copy.wait()
+
     flat = tracer[...].reshape(cells, width)
     table[...] = jnp.concatenate(split3(flat), axis=0).T.astype(BF16)
 
@@ -352,9 +375,16 @@
     return pl.pallas_call(
         functools.partial(kernel, devices, cap),
         out_shape=jax.ShapeDtypeStruct(tracer.shape, F32),
-        in_specs=[pl.BlockSpec(memory_space=vmem)] * 6,
+        in_specs=[pl.BlockSpec(memory_space=pltpu.HBM)] * 6,
         out_specs=pl.BlockSpec(memory_space=vmem),
         scratch_shapes=[
+            vmem(tracer.shape, F32),
+            vmem((elems, points), F32),
+            vmem((elems, points), F32),
+            vmem((elems, points), jnp.int32),
+            vmem((elems, points), jnp.int32),
+            vmem((2, elems, points), F32),
+            dma((6,)),
             vmem((width, 3 * cells), BF16),
             *[vmem((elems, tracers, points), F32)] * 3,
             *[vmem((blocks, tracers, points), F32)] * 3,
@@ -372,7 +402,7 @@
             *[dma((devices,))] * 6,
         ],
         compiler_params=pltpu.CompilerParams(
-            collective_id=0, has_side_effects=True, vmem_limit_bytes=48 * 1024 * 1024
+            collective_id=0, has_side_effects=True, vmem_limit_bytes=64 * 1024 * 1024 - 65536
         ),
     )(
         tracer, old_mass, new_mass,

time: 40.5 us -> 37.6 us (0.928)
  local copies, waits for them, and re-layouts: 5.03 us -> 1.59 us
  Pallas kernels: 35.1 us -> 35.9 us
    unnamed x13 -> x1, local copies, waits for them, and re-layouts: 5.03 us -> 1.59 us
    pallas_call x1, Pallas kernels: 35.1 us -> 35.9 us  [body(): pl.pallas_call(functools.partial(kernel, devices, cap), out_shape=jax.Sha...]
where the time goes in v2:
time: 37.6 us; the launch traced here: 37.5 us
  Pallas kernels  35.9 us (95%)
  local copies, waits for them, and re-layouts  1.59 us (4%)
    pallas_call x1, Pallas kernels, body(): pl.pallas_call(functools.partial(kernel, devices, cap), out_shape=jax.Sha...  35.9 us
    unnamed x1, local copies, waits for them, and re-layouts  1.59 us

profile of v2, /device:TPU:0, one launch (start us, length us, event | category | flops | bytes accessed | tf_op | source)
XLA Modules:
  0.0 37.5 jit_solution(12611226908077396336)
XLA Ops:
  0.0 35.9 %shard_map.64 = f32[8,8,640]{2,1,0:T(8,128)} custom-call(f32[8,8,640]{2,1,0:T(8,128)} %tracer_in.1, f32[8,128]{1,0:T(8,128)} %old_in.1, f32[8,128]{1,0:T(8,128)} %new_in.1, s32[8,128]{1,0:T(8,128)} %bitcast.1, s32[8,128]{1,0:T(8,128)} %local_in.1, f32[2,8,128]{2,1,0:T(8,128)} %coord_in.1), custom_call_target="tpu_custom_call" | custom-call | tf_op jit(solution)/shard_map/pallas_call | solution.py:375
  35.9 1.6 %copy.8 = f32[8,8,640]{2,1,0:T(8,128)} copy(f32[8,8,640]{2,1,0:T(8,128)} %shard_map.64) | data formatting | bytes 327680

commit v3 on v2

--- a/solution.py
+++ b/solution.py
@@ -42,12 +42,6 @@
 def dot_nt(a, b, precision=None):
     return lax.dot_general(
         a, b, (((1,), (1,)), ((), ())), precision=precision, preferred_element_type=F32
-    )
-
-
-def dot_tn(a, b, precision=None):
-    return lax.dot_general(
-        a, b, (((0,), (0,)), ((), ())), precision=precision, preferred_element_type=F32
     )
 
 
@@ -185,10 +179,14 @@
         margin = 0.01 + 0.05 * (highest - lowest)
         return clipped, highest + margin - clipped, clipped - lowest + margin
 
-    def mass_sums(weights, clipped, upper, lower):
+    def weighted(mass, clipped, upper, lower):
         rest = jnp.zeros((points - 3 * tracers, points), F32)
-        terms = jnp.concatenate([-clipped, upper, lower, rest], axis=0)
-        return dot_nt(weights, terms, HIGHEST)
+        return jnp.concatenate([-clipped * mass, upper * mass, lower * mass, rest], axis=0)
+
+    def by_level(terms, here):
+        parts = jnp.concatenate(split3(terms), axis=0).astype(BF16)
+        found = dot_nt(parts, here.astype(F32).astype(BF16))
+        return found[:points] + found[points : 2 * points] + found[2 * points :]
 
     for i, value in enumerate(one_axis(coord[0]) + one_axis(coord[1])):
         la_home[i] = value.reshape(elems, 1, points)
@@ -202,10 +200,10 @@
             fields[e], [la_home[i, e] for i in range(4)], [la_home[4 + i, e] for i in range(4)]
         )
         home_c[e], home_u[e], home_l[e] = results
-        weights = jnp.where(at_level, fields[elems + e], 0.0)
-        return sums + mass_sums(weights, *results)
-
-    sums = lax.fori_loop(0, elems, home_block, source)
+        return sums + weighted(fields[elems + e], *results)
+
+    sums = lax.fori_loop(0, elems, home_block, jnp.zeros((points, points), F32), unroll=2)
+    sums = by_level(sums, at_level)
 
     slot_ids = iota((devices * cap, points), 0).astype(F32)
     for e in range(elems):
@@ -243,9 +241,10 @@
             [la_far[i, first + 2] for i in range(4)],
         )
         far_c[b], far_u[b], far_l[b] = results
-        return sums + mass_sums(jnp.where(here, la_far[4, first + 3], 0.0), *results)
-
-    sums = lax.fori_loop(0, blocks, far_block, sums)
+        return sums + by_level(weighted(la_far[4, first + 3], *results), here)
+
+    sums = lax.fori_loop(0, blocks, far_block, sums, unroll=2)
+    sums = source + sums.T
 
     sum_out[...] = sums
     sum_in[pl.ds(me, 1)] = sums.reshape(1, levels, points)
@@ -274,8 +273,13 @@
     minus = jnp.where(inside, jnp.minimum(total, 0.0) / jnp.where(inside, down_total, 1.0), 0.0)
     factors = plus + pltpu.roll(minus, tracers, 1)
 
-    def fix(here, clipped, upper, lower):
-        by_lane = dot_tn(factors, here.astype(F32), HIGHEST)
+    factors = jnp.concatenate(split3(factors), axis=0).T.astype(BF16)
+
+    def spread_factors(here):
+        thrice = jnp.concatenate([here.astype(F32)] * 3, axis=0).astype(BF16)
+        return jnp.dot(factors, thrice, preferred_element_type=F32)
+
+    def fix(by_lane, clipped, upper, lower):
         return clipped + by_lane[:tracers] * upper + by_lane[tracers : 2 * tracers] * lower
 
     def answer(to, source):
@@ -306,7 +310,7 @@
     def send_block(turn, carry):
         b = lax.rem(turn + lax.div(me, group), blocks)
         _, here = slot_level(b)
-        fixed = fix(here, far_c[b], far_u[b], far_l[b])
+        fixed = fix(spread_factors(here), far_c[b], far_u[b], far_l[b])
         tiles = swap_blocks([fixed[8 * t : 8 * t + 8] for t in range(group)])
         last = fixed[8 * group :]
         for i in range(group):
@@ -320,13 +324,15 @@
 
         return carry
 
-    lax.fori_loop(0, blocks, send_block, 0)
+    lax.fori_loop(0, blocks, send_block, 0, unroll=2)
+
+    home_factors = spread_factors(at_level)
 
     def home_fix(e, carry):
-        home_c[e] = fix(at_level, home_c[e], home_u[e], home_l[e])
+        home_c[e] = fix(home_factors, home_c[e], home_u[e], home_l[e])
         return carry
 
-    lax.fori_loop(0, elems, home_fix, 0)
+    lax.fori_loop(0, elems, home_fix, 0, unroll=2)
     ans_in[pl.ds(me, 1)] = jnp.zeros((1, 16, points), F32)
 
     @pl.loop(1, devices)

time: 37.6 us -> 32.6 us (0.87)
  Pallas kernels: 35.9 us -> 30.7 us
    pallas_call x1, Pallas kernels: 35.9 us -> 30.7 us  [body(): pl.pallas_call(functools.partial(kernel, devices, cap), out_shape=jax.Sha...]
where the time goes in v3:
time: 32.6 us; the launch traced here: 32.3 us
  Pallas kernels  30.7 us (94%)
  local copies, waits for them, and re-layouts  1.59 us (5%)
    pallas_call x1, Pallas kernels, body(): pl.pallas_call(functools.partial(kernel, devices, cap), out_shape=jax.Sha...  30.7 us
    unnamed x1, local copies, waits for them, and re-layouts  1.59 us

profile of v3, /device:TPU:0, one launch (start us, length us, event | category | flops | bytes accessed | tf_op | source)
XLA Modules:
  0.0 32.3 jit_solution(7732433184443979289)
XLA Ops:
  0.0 30.7 %shard_map.64 = f32[8,8,640]{2,1,0:T(8,128)} custom-call(f32[8,8,640]{2,1,0:T(8,128)} %tracer_in.1, f32[8,128]{1,0:T(8,128)} %old_in.1, f32[8,128]{1,0:T(8,128)} %new_in.1, s32[8,128]{1,0:T(8,128)} %bitcast.1, s32[8,128]{1,0:T(8,128)} %local_in.1, f32[2,8,128]{2,1,0:T(8,128)} %coord_in.1), custom_call_target="tpu_custom_call" | custom-call | tf_op jit(solution)/shard_map/pallas_call | solution.py:381
  30.7 1.6 %copy.8 = f32[8,8,640]{2,1,0:T(8,128)} copy(f32[8,8,640]{2,1,0:T(8,128)} %shard_map.64) | data formatting | bytes 327680
